TPU v7x, 512 devices: a whole 4x4x16 slice. The times are simulated.
512 devices in a mesh: pipe: 16 (over z_lo, y), expert: 32 (over z_hi, x, core).
Axes of the slice: x: 4, y: 4, z: 16 (z_hi: 4, z_lo: 4; z = z_hi * 4 + z_lo), core: 2. Of those that a mesh axis runs over, the one named last changes fastest.
Arguments:
- act_prev: bfloat16 [16, 2048, 4096], P('pipe', 'expert'), may hold values from -6 to 6
- fwd_routes: int32 [16, 2048, 1], P('pipe', 'expert'), may hold values from 0 to 3; in each aligned block of 64 rows (0 to 63, 64 to 127, ..., all dimensions but the last counted through in order) at most 24 rows name the same one
- fwd_gates: float32 [16, 2048, 1], P('pipe', 'expert'), may hold values from 0.25 to 1.5
- saved_input: bfloat16 [16, 2048, 4096], P('pipe', 'expert'), may hold values from -6 to 6
- grad_prev: bfloat16 [16, 2048, 4096], P('pipe', 'expert'), may hold values from -6 to 6
- bwd_routes: int32 [16, 2048, 1], P('pipe', 'expert'), may hold values from 0 to 3; in each aligned block of 64 rows (0 to 63, 64 to 127, ..., all dimensions but the last counted through in order) at most 24 rows name the same one
- bwd_gates: float32 [16, 2048, 1], P('pipe', 'expert'), may hold values from 0.25 to 1.5
- norm_gain: float32 [16, 4096], P('pipe'), may hold values from 0.1 to 1.9
- w_up: bfloat16 [16, 32, 1024, 512], P('pipe', 'expert'), may hold values from -0.09375 to 0.09375
- w_down: bfloat16 [16, 32, 1024, 512], P('pipe', 'expert'), may hold values from -0.1875 to 0.1875
Outputs:
- section_out: bfloat16 [16, 2048, 4096], P('pipe', 'expert')
- input_grad: bfloat16 [16, 2048, 4096], P('pipe', 'expert')
Inputs may be any that keep to these rules, and one draw needn't show every extreme that they name: `fwd_routes`: the 1 ids of a token differ; among the 64 rows of one device (aligned blocks) no id is named by more than 24 rows, a bound that some block reaches. `bwd_routes`: the 1 ids of a token differ; among the 64 rows of one device (aligned blocks) no id is named by more than 24 rows, a bound that some block reaches.
All inputs are finite; a program needn't handle non-finite values.
Results may differ from a plain program's by a relative error of at most 0.0054.
Values may be sent and summed in bfloat16 or wider, within the bound.
A program may use at most 64 MiB of HBM per device.

v0:
```python
import jax
import jax.numpy as jnp
from jax import lax
from jax.sharding import PartitionSpec as P


def from_partner(value, axis, apart):
    return lax.ppermute(value, axis, [(i, i ^ 1 << apart) for i in range(lax.axis_size(axis))])


def passed_along(value, axis, by):
    devices = lax.axis_size(axis)
    return lax.ppermute(value, axis, [(i, (i + by) % devices) for i in range(devices)])


def slot_targets(routes, n_experts, capacity):
    rows, picks = routes.shape
    flat = routes.reshape(-1)
    hot = (flat[:, None] == jnp.arange(n_experts, dtype=jnp.int32)[None, :]).astype(jnp.int32)
    before = jnp.cumsum(hot, axis=0) - hot
    place = jnp.sum(before * hot, axis=1)
    target = flat * capacity + place
    target_hot = (
        target[:, None] == jnp.arange(n_experts * capacity, dtype=jnp.int32)[None, :]
    ).astype(jnp.bfloat16)
    return target_hot.reshape(rows, picks, n_experts, capacity)


def normalize(values, gain):
    scale = lax.rsqrt(jnp.mean(values * values, axis=-1, keepdims=True) + 1e-06)
    return values * scale * gain


def pack_rows(targets, values, hsplit):
    tok_rows, picks, n_experts, capacity = targets.shape
    choose = jnp.sum(targets, axis=1)
    split_values = values.reshape(tok_rows, hsplit, values.shape[1] // hsplit)
    packed = jnp.einsum("tec,thd->ehcd", choose, split_values, preferred_element_type=jnp.float32)
    return packed.reshape(n_experts * hsplit, capacity, split_values.shape[2]).astype(jnp.bfloat16)


def pack_picks(targets, values, hsplit):
    tok_rows, picks, n_experts, capacity = targets.shape
    split_values = values.reshape(tok_rows, picks, hsplit, values.shape[2] // hsplit)
    packed = jnp.einsum(
        "tkec,tkhd->ehcd", targets, split_values, preferred_element_type=jnp.float32
    )
    return packed.reshape(n_experts * hsplit, capacity, split_values.shape[3]).astype(jnp.bfloat16)


def unpack_gated(targets, gates, back, hsplit):
    tok_rows, picks, n_experts, capacity = targets.shape
    blocks = back.reshape(n_experts, hsplit, capacity, back.shape[2])
    rows_out = jnp.einsum("tkec,ehcd->tkhd", targets, blocks, preferred_element_type=jnp.float32)
    summed = jnp.sum(rows_out * gates[:, :, None, None], axis=1)
    return summed.reshape(tok_rows, hsplit * back.shape[2])


def unpack_rows(targets, back, hsplit):
    tok_rows, picks, n_experts, capacity = targets.shape
    choose = jnp.sum(targets, axis=1)
    blocks = back.reshape(n_experts, hsplit, capacity, back.shape[2])
    rows_out = jnp.einsum("tec,ehcd->thd", choose, blocks, preferred_element_type=jnp.float32)
    return rows_out.reshape(tok_rows, hsplit * back.shape[2])


def reduce_shares(parts, position, levels):
    current = parts
    for level in reversed(range(levels)):
        halves = current.reshape((2, current.shape[0] // 2) + current.shape[1:])
        own_bit = position // 2**level % 2
        kept = jnp.where(own_bit == 0, halves[0], halves[1])
        given = jnp.where(own_bit == 0, halves[1], halves[0])
        current = kept + from_partner(given, "expert", level)
    return current[0]


def collect_shares(piece, position, levels):
    current = piece[None]
    for level in range(levels):
        partner = from_partner(current, "expert", level)
        own_bit = position // 2**level % 2
        current = jnp.where(
            own_bit == 0,
            jnp.concatenate([current, partner], axis=0),
            jnp.concatenate([partner, current], axis=0),
        )
    return current


def silu_slope(hidden):
    sigma = jax.nn.sigmoid(hidden)
    return sigma * (1.0 + hidden * (1.0 - sigma))


def expert_forward(received, up_local, down_local, position, levels):
    rows = received.reshape(-1, received.shape[2])
    hidden_parts = jnp.einsum("rd,hsd->hrs", rows, up_local, preferred_element_type=jnp.float32)
    hidden_share = reduce_shares(hidden_parts, position, levels)
    active_share = jax.nn.silu(hidden_share).astype(jnp.bfloat16)
    active_full = collect_shares(active_share, position, levels)
    answer = jnp.einsum(
        "hrs,hsd->rd", active_full, down_local, preferred_element_type=jnp.float32
    ).astype(jnp.bfloat16)
    return answer.reshape(received.shape)


def expert_backward(received_rows, received_cot, up_local, down_local, position, levels):
    rows = received_rows.reshape(-1, received_rows.shape[2])
    cotangent = received_cot.reshape(-1, received_cot.shape[2])
    hidden_parts = jnp.einsum("rd,hsd->hrs", rows, up_local, preferred_element_type=jnp.float32)
    active_parts = jnp.einsum(
        "rd,hsd->hrs", cotangent, down_local, preferred_element_type=jnp.float32
    )
    summed = reduce_shares(jnp.stack([hidden_parts, active_parts], axis=1), position, levels)
    d_hidden = (summed[1] * silu_slope(summed[0])).astype(jnp.bfloat16)
    d_full = collect_shares(d_hidden, position, levels)
    answer = jnp.einsum("hrs,hsd->rd", d_full, up_local, preferred_element_type=jnp.float32).astype(
        jnp.bfloat16
    )
    return answer.reshape(received_rows.shape)


def local(
    act_prev,
    fwd_routes,
    fwd_gates,
    saved_input,
    grad_prev,
    bwd_routes,
    bwd_gates,
    norm_gain,
    w_up,
    w_down,
):
    groups = lax.axis_size("expert")
    levels = min(3, groups // 8)
    hsplit = 2**levels
    n_experts = groups // hsplit
    tok_rows = act_prev.shape[1]
    capacity = max(2, 3 * tok_rows * fwd_routes.shape[2] // (2 * n_experts))
    hidden_units = w_up.shape[2]
    slice_width = w_up.shape[3]
    share_units = hidden_units // hsplit
    gain = norm_gain[0]
    up_local = w_up[0, 0].reshape(hsplit, share_units, slice_width)
    down_local = w_down[0, 0].reshape(hsplit, share_units, slice_width)
    position = lax.axis_index("expert")
    arrived = passed_along(act_prev, "pipe", 1)[0]
    upstream = passed_along(grad_prev, "pipe", -1)[0]
    targets = slot_targets(fwd_routes[0], n_experts, capacity)
    normed = normalize(arrived.astype(jnp.float32), gain).astype(jnp.bfloat16)
    sent = pack_rows(targets, normed, hsplit)
    saved = saved_input[0].astype(jnp.float32)
    targets_b = slot_targets(bwd_routes[0], n_experts, capacity)
    normed_b = normalize(saved, gain).astype(jnp.bfloat16)
    sent_rows = pack_rows(targets_b, normed_b, hsplit)
    gated = (upstream.astype(jnp.float32)[:, None, :] * bwd_gates[0][:, :, None]).astype(
        jnp.bfloat16
    )
    sent_cot = pack_picks(targets_b, gated, hsplit)
    received = lax.all_to_all(sent, "expert", split_axis=0, concat_axis=0, tiled=True)
    fwd_results = expert_forward(received, up_local, down_local, position, levels)
    fwd_back = lax.all_to_all(fwd_results, "expert", split_axis=0, concat_axis=0, tiled=True)
    recv_rows, recv_cot = (
        lax.all_to_all(sent_rows, "expert", split_axis=0, concat_axis=0, tiled=True),
        lax.all_to_all(sent_cot, "expert", split_axis=0, concat_axis=0, tiled=True),
    )
    bwd_results = expert_backward(recv_rows, recv_cot, up_local, down_local, position, levels)
    bwd_back = lax.all_to_all(bwd_results, "expert", split_axis=0, concat_axis=0, tiled=True)
    section_out = (
        arrived.astype(jnp.float32) + unpack_gated(targets, fwd_gates[0], fwd_back, hsplit)
    ).astype(jnp.bfloat16)
    d_normed = unpack_rows(targets_b, bwd_back, hsplit)
    _, pull = jax.vjp(lambda values: normalize(values, gain), saved)
    d_input = pull(d_normed)[0]
    input_grad = (upstream.astype(jnp.float32) + d_input).astype(jnp.bfloat16)
    return (section_out[None], input_grad[None])


def solution(mesh):
    return jax.shard_map(
        local,
        mesh=mesh,
        in_specs=(
            P("pipe", "expert", None),
            P("pipe", "expert", None),
            P("pipe", "expert", None),
            P("pipe", "expert", None),
            P("pipe", "expert", None),
            P("pipe", "expert", None),
            P("pipe", "expert", None),
            P("pipe", None),
            P("pipe", "expert", None, None),
            P("pipe", "expert", None, None),
        ),
        out_specs=(P("pipe", "expert", None), P("pipe", "expert", None)),
        check_vma=False,
    )
```

profile of v0, /device:TPU:57, one launch (start us, length us, event | category | flops | bytes accessed | tf_op | source)
XLA Modules:
  0.0 482.7 jit_solution(4155744060432589964)
XLA Ops:
  3.1 1.2 fusion.22
  4.9 1.4 reduce.4
  6.3 1.2 copy.30
  9.4 17.5 %all-to-all-start.2 = ((bf16[32,24,512]{2,1,0:T(8,128)(2,1)}), bf16[32,24,512]{2,1,0:T(8,128)(2,1)S(1)}, u32[]{:S(2)}, u32[]{:S(2)}) async-start(bf16[32,24,512]{2,1,0:T(8,128)(2,1)} %bitcast.24), calls=%async_computation.2 | async-start | bytes 1572864 | tf_op jit(solution)/shard_map/all_to_all | solution.py:166
  26.9 2.3 collective-permute-start
  29.5 42.6 %collective-permute-done = bf16[1,64,4096]{2,1,0:T(8,128)(2,1)S(1)} collective-permute-done((bf16[1,64,4096]{2,1,0:T(8,128)(2,1)S(1)}, bf16[1,64,4096]{2,1,0:T(8,128)(2,1)S(1)}, u32[]{:S(2)}, u32[]{:S(2)}) %collective-permute-start) | collective-permute-done | bytes 524320 | tf_op jit(solution)/shard_map/ppermute | solution.py:13
  74.4 8.4 %all-to-all-done.2 = bf16[32,24,512]{2,1,0:T(8,128)(2,1)S(1)} async-done(((bf16[32,24,512]{2,1,0:T(8,128)(2,1)}), bf16[32,24,512]{2,1,0:T(8,128)(2,1)S(1)}, u32[]{:S(2)}, u32[]{:S(2)}) %all-to-all-start.2) | async-done | bytes 786464 | tf_op jit(solution)/shard_map/all_to_all | solution.py:166
  82.8 5.7 %all-to-all-start = ((bf16[32,24,512]{2,1,0:T(8,128)(2,1)}), bf16[32,24,512]{2,1,0:T(8,128)(2,1)S(1)}, u32[]{:S(2)}, u32[]{:S(2)}) async-start(bf16[32,24,512]{2,1,0:T(8,128)(2,1)} %bitcast.5), calls=%async_computation | async-start | bytes 1572864 | tf_op jit(solution)/shard_map/all_to_all | solution.py:162
  88.5 1.9 collective-permute-start.7
  90.4 45.1 %collective-permute-done.7 = bf16[1,64,4096]{2,1,0:T(8,128)(2,1)S(1)} collective-permute-done((bf16[1,64,4096]{2,1,0:T(8,128)(2,1)}, bf16[1,64,4096]{2,1,0:T(8,128)(2,1)S(1)}, u32[]{:S(2)}, u32[]{:S(2)}) %collective-permute-start.7) | collective-permute-done | bytes 524320 | tf_op jit(solution)/shard_map/ppermute | solution.py:13
  138.2 17.4 %all-to-all-start.3 = ((bf16[32,24,512]{2,1,0:T(8,128)(2,1)}), bf16[32,24,512]{2,1,0:T(8,128)(2,1)}, u32[]{:S(2)}, u32[]{:S(2)}) async-start(bf16[32,24,512]{2,1,0:T(8,128)(2,1)} %bitcast.33), calls=%async_computation.3 | async-start | bytes 1572864 | tf_op jit(solution)/shard_map/all_to_all | solution.py:167
  155.6 2.7 convolution_bitcast_fusion.2
  159.4 1.5 copy-done.1
  160.9 4.8 collective-permute-start.1
  165.7 20.9 %all-to-all-done.3 = bf16[32,24,512]{2,1,0:T(8,128)(2,1)} async-done(((bf16[32,24,512]{2,1,0:T(8,128)(2,1)}), bf16[32,24,512]{2,1,0:T(8,128)(2,1)}, u32[]{:S(2)}, u32[]{:S(2)}) %all-to-all-start.3) | async-done | bytes 786464 | tf_op jit(solution)/shard_map/all_to_all | solution.py:167
  186.6 2.6 convolution_bitcast_fusion.1
  189.3 2.2 broadcast_select_fusion
  191.9 5.5 %collective-permute-start.8 = (f32[4,2,768,128]{3,2,1,0:T(8,128)}, f32[4,2,768,128]{3,2,1,0:T(8,128)}, u32[]{:S(2)}, u32[]{:S(2)}) collective-permute-start(f32[4,2,768,128]{3,2,1,0:T(8,128)} %broadcast_select_fusion), channel_id=1, source_target_pairs={{0,4},{1,5},{2,6},{3,7},{4,0},{5,1},{6,2},{7,3},{8,12},{9,13},{10,... | collective-permute-start | bytes 9437192 | tf_op jit(solution)/shard_map/ppermute | solution.py:8
  197.5 8.6 %collective-permute-done.1 = f32[4,768,128]{2,1,0:T(8,128)} collective-permute-done((f32[4,768,128]{2,1,0:T(8,128)S(1)}, f32[4,768,128]{2,1,0:T(8,128)}, u32[]{:S(2)}, u32[]{:S(2)}) %collective-permute-start.1) | collective-permute-done | bytes 1572896 | tf_op jit(solution)/shard_map/ppermute | solution.py:8
  206.1 2.6 select_add_fusion.2
  209.7 3.3 collective-permute-start.2
  213.0 77.5 %collective-permute-done.2 = f32[2,768,128]{2,1,0:T(8,128)} collective-permute-done((f32[2,768,128]{2,1,0:T(8,128)}, f32[2,768,128]{2,1,0:T(8,128)}, u32[]{:S(2)}, u32[]{:S(2)}) %collective-permute-start.2) | collective-permute-done | bytes 786464 | tf_op jit(solution)/shard_map/ppermute | solution.py:8
  290.5 1.2 select_add_fusion.4
  291.8 3.1 collective-permute-start.3
  294.9 3.4 select_add_fusion
  298.5 3.1 collective-permute-start.9
  301.7 2.2 collective-permute-start.4
  304.0 1.1 collective-permute-done.4
  305.1 2.2 collective-permute-start.5
  307.3 37.5 %collective-permute-done.5 = bf16[2,768,128]{2,1,0:T(8,128)(2,1)S(1)} collective-permute-done((bf16[2,768,128]{2,1,0:T(8,128)(2,1)S(1)}, bf16[2,768,128]{2,1,0:T(8,128)(2,1)S(1)}, u32[]{:S(2)}, u32[]{:S(2)}) %collective-permute-start.5) | collective-permute-done | bytes 393248 | tf_op jit(solution)/shard_map/ppermute | solution.py:8
  345.0 3.8 collective-permute-start.6
  349.9 3.0 collective-permute-start.10
  352.9 13.7 %collective-permute-done.6 = bf16[4,768,128]{2,1,0:T(8,128)(2,1)S(1)} collective-permute-done((bf16[4,768,128]{2,1,0:T(8,128)(2,1)S(1)}, bf16[4,768,128]{2,1,0:T(8,128)(2,1)S(1)}, u32[]{:S(2)}, u32[]{:S(2)}) %collective-permute-start.6) | collective-permute-done | bytes 786464 | tf_op jit(solution)/shard_map/ppermute | solution.py:8
  366.6 1.9 bitcast_convert_fusion.1
  368.5 14.2 %all-to-all-start.1 = ((bf16[32,24,512]{2,1,0:T(8,128)(2,1)}), bf16[32,24,512]{2,1,0:T(8,128)(2,1)}, u32[]{:S(2)}, u32[]{:S(2)}) async-start(bf16[32,24,512]{2,1,0:T(8,128)(2,1)} %bitcast.152), calls=%async_computation.1 | async-start | bytes 1572864 | tf_op jit(solution)/shard_map/all_to_all | solution.py:164
  382.8 1.2 select_add_fusion.3
  384.2 2.2 collective-permute-start.11
  387.6 3.3 collective-permute-start.12
  390.9 11.7 %collective-permute-done.12 = bf16[2,768,128]{2,1,0:T(8,128)(2,1)S(1)} collective-permute-done((bf16[2,768,128]{2,1,0:T(8,128)(2,1)S(1)}, bf16[2,768,128]{2,1,0:T(8,128)(2,1)S(1)}, u32[]{:S(2)}, u32[]{:S(2)}) %collective-permute-start.12) | collective-permute-done | bytes 393248 | tf_op jit(solution)/shard_map/ppermute | solution.py:8
  402.7 4.5 collective-permute-start.13
  407.2 19.6 %collective-permute-done.13 = bf16[4,768,128]{2,1,0:T(8,128)(2,1)S(1)} collective-permute-done((bf16[4,768,128]{2,1,0:T(8,128)(2,1)S(1)}, bf16[4,768,128]{2,1,0:T(8,128)(2,1)S(1)}, u32[]{:S(2)}, u32[]{:S(2)}) %collective-permute-start.13) | collective-permute-done | bytes 786464 | tf_op jit(solution)/shard_map/ppermute | solution.py:8
  426.9 1.9 bitcast_convert_fusion
  428.7 14.9 %all-to-all-start.4 = ((bf16[32,24,512]{2,1,0:T(8,128)(2,1)}), bf16[32,24,512]{2,1,0:T(8,128)(2,1)S(1)}, u32[]{:S(2)}, u32[]{:S(2)}) async-start(bf16[32,24,512]{2,1,0:T(8,128)(2,1)} %bitcast.41), calls=%async_computation.4 | async-start | bytes 1572864 | tf_op jit(solution)/shard_map/all_to_all | solution.py:170
  443.6 1.6 fusion.16
  445.2 1.6 copy.19
  446.8 1.4 reshape.307
  449.1 30.8 %all-to-all-done.4 = bf16[32,24,512]{2,1,0:T(8,128)(2,1)S(1)} async-done(((bf16[32,24,512]{2,1,0:T(8,128)(2,1)}), bf16[32,24,512]{2,1,0:T(8,128)(2,1)S(1)}, u32[]{:S(2)}, u32[]{:S(2)}) %all-to-all-start.4) | async-done | bytes 786464 | tf_op jit(solution)/shard_map/all_to_all | solution.py:170
  481.6 1.1 fusion.35
  (74 shorter events, 18.3 us)
Async XLA Ops:
  0.6 154.9 %copy-start = (bf16[1,1,1024,512]{3,2,1,0:T(8,128)(2,1)S(1)}, bf16[1,1,1024,512]{3,2,1,0:T(8,128)(2,1)}, u32[]{:S(2)}) copy-start(bf16[1,1,1024,512]{3,2,1,0:T(8,128)(2,1)} %param.18) | copy-start | bytes 3145732
  8.3 18.5 %copy-start.13 = (bf16[1,64,4096]{2,1,0:T(8,128)(2,1)S(1)}, bf16[1,64,4096]{2,1,0:T(8,128)(2,1)}, u32[]{:S(2)}) copy-start(bf16[1,64,4096]{2,1,0:T(8,128)(2,1)} %param.10) | copy-start | bytes 1572868
  8.4 20.8 %copy-start.9 = (s32[1,64,1]{1,2,0:T(1,128)S(1)}, s32[1,64,1]{1,2,0:T(1,128)}, u32[]{:S(2)}) copy-start(s32[1,64,1]{1,2,0:T(1,128)} %param.11) | copy-start | bytes 772
  9.4 73.4 %all-to-all-start.2 = ((bf16[32,24,512]{2,1,0:T(8,128)(2,1)}), bf16[32,24,512]{2,1,0:T(8,128)(2,1)S(1)}, u32[]{:S(2)}, u32[]{:S(2)}) async-start(bf16[32,24,512]{2,1,0:T(8,128)(2,1)} %bitcast.24), calls=%async_computation.2 | async-start | bytes 1572864 | tf_op jit(solution)/shard_map/all_to_all | solution.py:166
  26.9 45.3 %collective-permute-start = (bf16[1,64,4096]{2,1,0:T(8,128)(2,1)S(1)}, bf16[1,64,4096]{2,1,0:T(8,128)(2,1)S(1)}, u32[]{:S(2)}, u32[]{:S(2)}) collective-permute-start(bf16[1,64,4096]{2,1,0:T(8,128)(2,1)S(1)} %copy-done.13), channel_id=1, source_target_pairs={{0,32},{32,64},{64,96},{96,128},{128,160},{160,192},{192,224},{224... | collective-permute-start | bytes 1572872 | tf_op jit(solution)/shard_map/ppermute | solution.py:13
  82.8 53.5 %copy-start.10 = (f32[1,64,1]{1,2,0:T(1,128)S(1)}, f32[1,64,1]{1,2,0:T(1,128)}, u32[]{:S(2)}) copy-start(f32[1,64,1]{1,2,0:T(1,128)} %param.16) | copy-start | bytes 772
  82.8 55.3 %all-to-all-start = ((bf16[32,24,512]{2,1,0:T(8,128)(2,1)}), bf16[32,24,512]{2,1,0:T(8,128)(2,1)S(1)}, u32[]{:S(2)}, u32[]{:S(2)}) async-start(bf16[32,24,512]{2,1,0:T(8,128)(2,1)} %bitcast.5), calls=%async_computation | async-start | bytes 1572864 | tf_op jit(solution)/shard_map/all_to_all | solution.py:162
  88.5 47.1 %collective-permute-start.7 = (bf16[1,64,4096]{2,1,0:T(8,128)(2,1)}, bf16[1,64,4096]{2,1,0:T(8,128)(2,1)S(1)}, u32[]{:S(2)}, u32[]{:S(2)}) collective-permute-start(bf16[1,64,4096]{2,1,0:T(8,128)(2,1)} %param.14), channel_id=1, source_target_pairs={{0,480},{32,0},{64,32},{96,64},{128,96},{160,128},{192,160},{224,1... | collective-permute-start | bytes 1572872 | tf_op jit(solution)/shard_map/ppermute | solution.py:13
  135.6 0.8 copy-start.6
  138.2 48.5 %all-to-all-start.3 = ((bf16[32,24,512]{2,1,0:T(8,128)(2,1)}), bf16[32,24,512]{2,1,0:T(8,128)(2,1)}, u32[]{:S(2)}, u32[]{:S(2)}) async-start(bf16[32,24,512]{2,1,0:T(8,128)(2,1)} %bitcast.33), calls=%async_computation.3 | async-start | bytes 1572864 | tf_op jit(solution)/shard_map/all_to_all | solution.py:167
  159.2 1.6 copy-start.1
  160.9 45.2 %collective-permute-start.1 = (f32[4,768,128]{2,1,0:T(8,128)S(1)}, f32[4,768,128]{2,1,0:T(8,128)}, u32[]{:S(2)}, u32[]{:S(2)}) collective-permute-start(f32[4,768,128]{2,1,0:T(8,128)S(1)} %slice_select_fusion.1), channel_id=1, source_target_pairs={{0,4},{1,5},{2,6},{3,7},{4,0},{5,1},{6,2},{7,3},{8,12},{9,13},{10,... | collective-permute-start | bytes 4718600 | tf_op jit(solution)/shard_map/ppermute | solution.py:8
  186.6 2.6 copy-start.2
  189.2 2.6 copy-start.4
  191.9 103.0 %collective-permute-start.8 = (f32[4,2,768,128]{3,2,1,0:T(8,128)}, f32[4,2,768,128]{3,2,1,0:T(8,128)}, u32[]{:S(2)}, u32[]{:S(2)}) collective-permute-start(f32[4,2,768,128]{3,2,1,0:T(8,128)} %broadcast_select_fusion), channel_id=1, source_target_pairs={{0,4},{1,5},{2,6},{3,7},{4,0},{5,1},{6,2},{7,3},{8,12},{9,13},{10,... | collective-permute-start | bytes 9437192 | tf_op jit(solution)/shard_map/ppermute | solution.py:8
  209.7 80.8 %collective-permute-start.2 = (f32[2,768,128]{2,1,0:T(8,128)}, f32[2,768,128]{2,1,0:T(8,128)}, u32[]{:S(2)}, u32[]{:S(2)}) collective-permute-start(f32[2,768,128]{2,1,0:T(8,128)} %slice_select_fusion.3), channel_id=1, source_target_pairs={{0,2},{1,3},{2,0},{3,1},{4,6},{5,7},{6,4},{7,5},{8,10},{9,11},{10,... | collective-permute-start | bytes 2359304 | tf_op jit(solution)/shard_map/ppermute | solution.py:8
  213.0 81.9 %copy-start.3 = (f32[8,1,768,128]{3,2,1,0:T(8,128)S(1)}, f32[8,1,768,128]{3,2,1,0:T(8,128)}, u32[]{:S(2)}) copy-start(f32[8,1,768,128]{3,2,1,0:T(8,128)} %convolution_bitcast_fusion.2) | copy-start | bytes 9437188
  291.8 9.8 %collective-permute-start.3 = (f32[1,768,128]{2,1,0:T(8,128)S(1)}, f32[1,768,128]{2,1,0:T(8,128)S(1)}, u32[]{:S(2)}, u32[]{:S(2)}) collective-permute-start(f32[1,768,128]{2,1,0:T(8,128)S(1)} %slice_select_fusion.4), channel_id=1, source_target_pairs={{0,1},{1,0},{2,3},{3,2},{4,5},{5,4},{6,7},{7,6},{8,9},{9,8},{10,11... | collective-permute-start | bytes 1179656 | tf_op jit(solution)/shard_map/ppermute | solution.py:8
  298.5 50.2 %collective-permute-start.9 = (f32[2,2,768,128]{3,2,1,0:T(8,128)S(1)}, f32[2,2,768,128]{3,2,1,0:T(8,128)S(1)}, u32[]{:S(2)}, u32[]{:S(2)}) collective-permute-start(f32[2,2,768,128]{3,2,1,0:T(8,128)S(1)} %slice_select_fusion), channel_id=1, source_target_pairs={{0,2},{1,3},{2,0},{3,1},{4,6},{5,7},{6,4},{7,5},{8,10},{9,11},{10,... | collective-permute-start | bytes 4718600 | tf_op jit(solution)/shard_map/ppermute | solution.py:8
  301.7 3.3 collective-permute-start.4
  305.1 39.7 %collective-permute-start.5 = (bf16[2,768,128]{2,1,0:T(8,128)(2,1)S(1)}, bf16[2,768,128]{2,1,0:T(8,128)(2,1)S(1)}, u32[]{:S(2)}, u32[]{:S(2)}) collective-permute-start(bf16[2,768,128]{2,1,0:T(8,128)(2,1)S(1)} %maximum_select_fusion.10), channel_id=1, source_target_pairs={{0,2},{1,3},{2,0},{3,1},{4,6},{5,7},{6,4},{7,5},{8,10},{9,11},{10,... | collective-permute-start | bytes 1179656 | tf_op jit(solution)/shard_map/ppermute | solution.py:8
  345.0 21.7 %collective-permute-start.6 = (bf16[4,768,128]{2,1,0:T(8,128)(2,1)S(1)}, bf16[4,768,128]{2,1,0:T(8,128)(2,1)S(1)}, u32[]{:S(2)}, u32[]{:S(2)}) collective-permute-start(bf16[4,768,128]{2,1,0:T(8,128)(2,1)S(1)} %maximum_select_fusion.8), channel_id=1, source_target_pairs={{0,4},{1,5},{2,6},{3,7},{4,0},{5,1},{6,2},{7,3},{8,12},{9,13},{10,... | collective-permute-start | bytes 2359304 | tf_op jit(solution)/shard_map/ppermute | solution.py:8
  349.0 17.7 %copy-start.12 = (bf16[1,1,1024,512]{3,2,1,0:T(8,128)(2,1)S(1)}, bf16[1,1,1024,512]{3,2,1,0:T(8,128)(2,1)}, u32[]{:S(2)}) copy-start(bf16[1,1,1024,512]{3,2,1,0:T(8,128)(2,1)} %param.19) | copy-start | bytes 3145732
  349.9 32.8 %collective-permute-start.10 = (f32[1,2,768,128]{3,2,1,0:T(8,128)}, f32[1,2,768,128]{3,2,1,0:T(8,128)}, u32[]{:S(2)}, u32[]{:S(2)}) collective-permute-start(f32[1,2,768,128]{3,2,1,0:T(8,128)} %slice_select_fusion.2), channel_id=1, source_target_pairs={{0,1},{1,0},{2,3},{3,2},{4,5},{5,4},{6,7},{7,6},{8,9},{9,8},{10,11... | collective-permute-start | bytes 2359304 | tf_op jit(solution)/shard_map/ppermute | solution.py:8
  368.5 60.2 %all-to-all-start.1 = ((bf16[32,24,512]{2,1,0:T(8,128)(2,1)}), bf16[32,24,512]{2,1,0:T(8,128)(2,1)}, u32[]{:S(2)}, u32[]{:S(2)}) async-start(bf16[32,24,512]{2,1,0:T(8,128)(2,1)} %bitcast.152), calls=%async_computation.1 | async-start | bytes 1572864 | tf_op jit(solution)/shard_map/all_to_all | solution.py:164
  384.2 3.3 collective-permute-start.11
  387.6 15.0 %collective-permute-start.12 = (bf16[2,768,128]{2,1,0:T(8,128)(2,1)S(1)}, bf16[2,768,128]{2,1,0:T(8,128)(2,1)S(1)}, u32[]{:S(2)}, u32[]{:S(2)}) collective-permute-start(bf16[2,768,128]{2,1,0:T(8,128)(2,1)S(1)} %maximum_select_fusion.11), channel_id=1, source_target_pairs={{0,2},{1,3},{2,0},{3,1},{4,6},{5,7},{6,4},{7,5},{8,10},{9,11},{10,... | collective-permute-start | bytes 1179656 | tf_op jit(solution)/shard_map/ppermute | solution.py:8
  402.7 24.1 %collective-permute-start.13 = (bf16[4,768,128]{2,1,0:T(8,128)(2,1)S(1)}, bf16[4,768,128]{2,1,0:T(8,128)(2,1)S(1)}, u32[]{:S(2)}, u32[]{:S(2)}) collective-permute-start(bf16[4,768,128]{2,1,0:T(8,128)(2,1)S(1)} %maximum_select_fusion.9), channel_id=1, source_target_pairs={{0,4},{1,5},{2,6},{3,7},{4,0},{5,1},{6,2},{7,3},{8,12},{9,13},{10,... | collective-permute-start | bytes 2359304 | tf_op jit(solution)/shard_map/ppermute | solution.py:8
  428.7 14.9 %copy-start.11 = (f32[1,64,1]{1,2,0:T(1,128)S(1)}, f32[1,64,1]{1,2,0:T(1,128)}, u32[]{:S(2)}) copy-start(f32[1,64,1]{1,2,0:T(1,128)} %param.12) | copy-start | bytes 772
  428.7 51.2 %all-to-all-start.4 = ((bf16[32,24,512]{2,1,0:T(8,128)(2,1)}), bf16[32,24,512]{2,1,0:T(8,128)(2,1)S(1)}, u32[]{:S(2)}, u32[]{:S(2)}) async-start(bf16[32,24,512]{2,1,0:T(8,128)(2,1)} %bitcast.41), calls=%async_computation.4 | async-start | bytes 1572864 | tf_op jit(solution)/shard_map/all_to_all | solution.py:170
  479.9 1.0 copy-start.5
  479.9 1.0 copy-start.8
  480.5 1.1 copy-start.7
where the time goes:
time: 484 us; the launch traced here: 483 us
  waiting for transfers between devices  319 us (66%)
  starting transfers between devices  115 us (24%)
  other arithmetic  21.5 us (4%)
  matrix products  14.6 us (3%)
  local copies, waits for them, and re-layouts  11.8 us (2%)
    ppermute x12, waiting for transfers between devices, from_partner(): lax.ppermute(value, axis, [(i, i ^ 1 << apart) for i in range(lax.axis_si...  171 us
    ppermute x2, waiting for transfers between devices, passed_along(): lax.ppermute(value, axis, [(i, (i + by) % devices) for i in range(devices)])  87.8 us
    ppermute x12, starting transfers between devices, from_partner(): lax.ppermute(value, axis, [(i, i ^ 1 << apart) for i in range(lax.axis_si...  40.9 us
    all_to_all x1, waiting for transfers between devices, local(): lax.all_to_all(bwd_results, 'expert', split_axis=0, concat_axis=0, tiled=...  30.8 us
    all_to_all x1, waiting for transfers between devices, local(): lax.all_to_all(sent_cot, 'expert', split_axis=0, concat_axis=0, tiled=True)  20.9 us
    all_to_all x1, starting transfers between devices, local(): lax.all_to_all(sent_rows, 'expert', split_axis=0, concat_axis=0, tiled=True)  17.5 us
    all_to_all x1, starting transfers between devices, local(): lax.all_to_all(sent_cot, 'expert', split_axis=0, concat_axis=0, tiled=True)  17.4 us
    all_to_all x1, starting transfers between devices, local(): lax.all_to_all(bwd_results, 'expert', split_axis=0, concat_axis=0, tiled=...  14.9 us
  transfers between devices with their start and end apart: 19, of which 13 were waited for; matrix products, arithmetic and copies ran while one was open for 7% of the time, Pallas kernels for 0%

commit v1 on v0

v1 whole, which is shorter than its diff:
```python
import functools

import jax
import jax.numpy as jnp
from jax import lax
from jax.experimental import pallas as pl
from jax.experimental.pallas import tpu as pltpu
from jax.sharding import PartitionSpec as P

MESH = pl.DeviceIdType.MESH
EPS = 1e-06
ROWS, COT, FWD = 0, 1, 2
DROW, EOUT = 0, 1
TRANS_RHS = (((1,), (1,)), ((), ()))


def slot_masks(routes, here, n_experts, capacity):
    tokens = routes.shape[0]
    relative = lax.rem(routes - here + n_experts, n_experts).astype(jnp.float32)
    down = lax.broadcasted_iota(jnp.int32, (tokens, tokens), 0)
    across = lax.broadcasted_iota(jnp.int32, (tokens, tokens), 1)
    as_row = jnp.sum(jnp.where(down == across, relative, 0.0), axis=0, keepdims=True)
    same = jnp.where(relative == as_row, 1.0, 0.0)
    rank_col = jnp.sum(jnp.where(across < down, same, 0.0), axis=1, keepdims=True)
    rank_row = jnp.sum(jnp.where(down < across, same, 0.0), axis=0, keepdims=True)
    slots = n_experts * capacity
    target_col = (relative * capacity + rank_col).astype(jnp.int32)
    target_row = (as_row * capacity + rank_row).astype(jnp.int32)
    slot_of_col = lax.broadcasted_iota(jnp.int32, (tokens, slots), 1)
    slot_of_row = lax.broadcasted_iota(jnp.int32, (slots, tokens), 0)
    gather = jnp.where(target_col == slot_of_col, 1.0, 0.0).astype(jnp.bfloat16)
    pack = jnp.where(target_row == slot_of_row, 1.0, 0.0).astype(jnp.bfloat16)
    return gather, pack


def kernel(
    sizes,
    act_ref,
    fwd_routes_ref,
    fwd_gates_ref,
    saved_ref,
    grad_ref,
    bwd_routes_ref,
    bwd_gates_ref,
    gain_ref,
    up_ref,
    down_ref,
    out_ref,
    dx_ref,
    x_buf,
    gy_buf,
    up_all,
    down_all,
    normed,
    snd,
    rcv,
    ret,
    bak,
    hid,
    dact,
    mid,
    dn,
    pipe_send,
    pipe_recv,
    w_send,
    w_recv,
    w_own,
    disp_send,
    disp_recv,
    ret_send,
    ret_recv,
):
    n_pipe, n_experts, n_x, cap, chunks, width = sizes
    tokens = saved_ref.shape[1]
    dim = saved_ref.shape[2]
    per_group = 2 * n_x
    pipe = lax.axis_index("pipe")
    place = lax.axis_index("expert")
    here = place // per_group
    spot = lax.rem(place, per_group)
    my_x, core = spot // 2, lax.rem(spot, 2)

    def spot_of(x, c):
        return lax.rem(x + n_x, n_x) * 2 + c

    def group_peer(offset):
        return (pipe, lax.rem(here + offset + n_experts, n_experts) * per_group + spot)

    right = (pipe, here * per_group + spot_of(my_x + 1, core))
    left = (pipe, here * per_group + spot_of(my_x - 1, core))
    sibling = (pipe, here * per_group + spot_of(my_x, 1 - core))
    later = (lax.rem(pipe + 1, n_pipe), place)
    earlier = (lax.rem(pipe + n_pipe - 1, n_pipe), place)

    barrier = pltpu.get_barrier_semaphore()
    peers = [right, left, sibling, later, earlier] + [group_peer(k) for k in range(1, n_experts)]
    for peer in peers:
        pl.semaphore_signal(barrier, inc=1, device_id=peer, device_id_type=MESH)

    def pipe_copy(i):
        src, dst, peer = ((act_ref.at[0], x_buf, later), (grad_ref.at[0], gy_buf, earlier))[i]
        return pltpu.make_async_remote_copy(
            src_ref=src,
            dst_ref=dst,
            send_sem=pipe_send.at[i],
            recv_sem=pipe_recv.at[i],
            device_id=peer,
            device_id_type=MESH,
        )

    def dispatch(which, c, k):
        return pltpu.make_async_remote_copy(
            src_ref=snd.at[which, c, k - 1],
            dst_ref=rcv.at[which, c, k],
            send_sem=disp_send.at[which, c, k - 1],
            recv_sem=disp_recv.at[which, c, k - 1],
            device_id=group_peer(k),
            device_id_type=MESH,
        )

    def give_back(which, c, k):
        return pltpu.make_async_remote_copy(
            src_ref=ret.at[which, c, k - 1],
            dst_ref=bak.at[which, c, k],
            send_sem=ret_send.at[which, c, k - 1],
            recv_sem=ret_recv.at[which, c, k - 1],
            device_id=group_peer(-k),
            device_id_type=MESH,
        )

    half = up_ref.shape[2] // 2
    first, second = pl.ds(0, half), pl.ds(half, half)
    spot_l, spot_r = spot_of(my_x - 1, core), spot_of(my_x + 1, core)
    spot_a = spot_of(my_x + 2, core)
    arrivals = [
        (spot_l, first),
        (spot_l, second),
        (spot_r, first),
        (spot_r, second),
        (spot_a, first),
        (spot_a, second),
    ]

    def weight_copy(m, i):
        own, everything = ((up_ref, up_all), (down_ref, down_all))[m]
        if i < 4:
            rows = (first, second)[i % 2]
            src, dst = own.at[0, 0, rows], everything.at[spot, rows]
            peer = right if i < 2 else left
        elif i == 4:
            src = dst = everything.at[spot_l, first]
            peer = right
        elif i == 5:
            src = dst = everything.at[spot_r, second]
            peer = left
        elif i == 6:
            src, dst, peer = own.at[0, 0], everything.at[spot], sibling
        else:
            at, rows = arrivals[i - 7]
            src = dst = everything.at[at, rows]
            peer = sibling
        return pltpu.make_async_remote_copy(
            src_ref=src,
            dst_ref=dst,
            send_sem=w_send.at[m, i],
            recv_sem=w_recv.at[m, i],
            device_id=peer,
            device_id_type=MESH,
        )

    own_copies = [
        pltpu.make_async_copy(up_ref.at[0, 0], up_all.at[spot], w_own.at[0]),
        pltpu.make_async_copy(down_ref.at[0, 0], down_all.at[spot], w_own.at[1]),
    ]
    for copy in own_copies:
        copy.start()

    def cols(h):
        return pl.ds(pl.multiple_of(h * width, width), width)

    def put_slots(c, low, high, remote, local):
        for k in range(n_experts):
            rows = slice(k * cap, (k + 1) * cap)
            piece = jnp.concatenate([low[rows], high[rows]], axis=0).astype(jnp.bfloat16)
            if k == 0:
                local[c, 0] = piece
            else:
                remote[c, k - 1] = piece

    def take_slots(buf, c):
        whole = [buf[c, k].astype(jnp.float32) for k in range(n_experts)]
        return [
            jnp.concatenate([w[j * cap : (j + 1) * cap] for w in whole], axis=0).astype(jnp.bfloat16)
            for j in range(2)
        ]

    def pack_piece(which, c, pack):
        low, high = [
            jnp.dot(pack, normed[:, cols(2 * c + j)], preferred_element_type=jnp.float32)
            for j in range(2)
        ]
        put_slots(c, low, high, snd.at[which], rcv.at[which])

    def send_piece(which, c):
        for k in range(1, n_experts):
            dispatch(which, c, k).start()

    def pack_and_send(which, pack):
        @pl.loop(0, chunks)
        def _(c):
            pack_piece(which, c, pack)
            send_piece(which, c)

    def scale_of(values):
        return lax.rsqrt(jnp.sum(values * values, axis=-1, keepdims=True) * (1.0 / dim) + EPS)

    gain = gain_ref[...]

    saved = saved_ref[0].astype(jnp.float32)
    scale_b = scale_of(saved)
    normed[...] = (saved * scale_b * gain).astype(jnp.bfloat16)
    gather_b, pack_b = slot_masks(bwd_routes_ref[0], here, n_experts, cap)

    @pl.loop(0, chunks)
    def _(c):
        pack_piece(ROWS, c, pack_b)

    pl.semaphore_wait(barrier, len(peers))

    pipe_copy(1).start()
    pipe_copy(0).start()

    @pl.loop(0, chunks)
    def _(c):
        send_piece(ROWS, c)

    for m in range(2):
        for i in (0, 3, 1, 2, 6):
            weight_copy(m, i).start()

    pipe_copy(1).wait_recv()
    normed[...] = (gy_buf[...].astype(jnp.float32) * bwd_gates_ref[0]).astype(jnp.bfloat16)
    pack_and_send(COT, pack_b)

    gather_f, pack_f = slot_masks(fwd_routes_ref[0], here, n_experts, cap)
    pipe_copy(0).wait_recv()
    x = x_buf[...].astype(jnp.float32)
    normed[...] = (x * scale_of(x) * gain).astype(jnp.bfloat16)
    pack_and_send(FWD, pack_f)

    def pass_on(m):
        weight_copy(m, 0).wait_recv()
        weight_copy(m, 4).start()
        weight_copy(m, 7).start()
        weight_copy(m, 3).wait_recv()
        weight_copy(m, 5).start()
        weight_copy(m, 10).start()
        for i in (1, 2, 4, 5):
            weight_copy(m, i).wait_recv()
            weight_copy(m, 7 + i).start()

    def have_weights(m):
        own_copies[m].wait()
        for i in range(6, 13):
            weight_copy(m, i).wait_recv()

    def into_hidden(which, weights, total):
        total[...] = jnp.zeros_like(total)

        @pl.loop(0, chunks)
        def _(c):
            for k in range(1, n_experts):
                dispatch(which, c, k).wait_recv()
            for j, rows in enumerate(take_slots(rcv.at[which], c)):
                total[...] += lax.dot_general(
                    rows, weights[2 * c + j], TRANS_RHS, preferred_element_type=jnp.float32
                )

    def out_of_hidden(which, weights):
        @pl.loop(0, chunks)
        def _(c):
            low, high = [
                jnp.dot(mid[...], weights[2 * c + j], preferred_element_type=jnp.float32)
                for j in range(2)
            ]
            put_slots(c, low, high, ret.at[which], bak.at[which])
            for k in range(1, n_experts):
                give_back(which, c, k).start()

    pass_on(0)
    have_weights(0)
    into_hidden(ROWS, up_all, hid)
    pass_on(1)
    have_weights(1)
    into_hidden(COT, down_all, dact)
    h = hid[...]
    sigma = 1.0 / (1.0 + jnp.exp(-h))
    mid[...] = (dact[...] * (sigma * (1.0 + h * (1.0 - sigma)))).astype(jnp.bfloat16)
    out_of_hidden(DROW, up_all)

    into_hidden(FWD, up_all, hid)
    h = hid[...]
    mid[...] = (h / (1.0 + jnp.exp(-h))).astype(jnp.bfloat16)
    out_of_hidden(EOUT, down_all)

    def from_slots(which, c, gather):
        for k in range(1, n_experts):
            give_back(which, c, k).wait_recv()
        return [
            jnp.dot(gather, rows, preferred_element_type=jnp.float32)
            for rows in take_slots(bak.at[which], c)
        ]

    def gradient_piece(c, total):
        for j, d in enumerate(from_slots(DROW, c, gather_b)):
            at = cols(2 * c + j)
            scaled = d * gain_ref[:, at]
            dn[:, at] = scaled
            total = total + jnp.sum(
                scaled * saved_ref[0, :, at].astype(jnp.float32), axis=-1, keepdims=True
            )
        return total

    total = lax.fori_loop(0, chunks, gradient_piece, jnp.zeros((tokens, 1), jnp.float32))
    pull = total * (1.0 / dim) * scale_b * scale_b * scale_b
    dx_ref[0] = (
        gy_buf[...].astype(jnp.float32)
        + (dn[...] * scale_b - saved_ref[0].astype(jnp.float32) * pull)
    ).astype(jnp.bfloat16)

    gates = fwd_gates_ref[0]

    @pl.loop(0, chunks)
    def _(c):
        for j, e in enumerate(from_slots(EOUT, c, gather_f)):
            at = cols(2 * c + j)
            out_ref[0, :, at] = (x_buf[:, at].astype(jnp.float32) + e * gates).astype(jnp.bfloat16)

    for i in range(2):
        pipe_copy(i).wait_send()
    for m in range(2):
        for i in range(13):
            weight_copy(m, i).wait_send()

    @pl.loop(0, chunks)
    def _(c):
        for k in range(1, n_experts):
            for which in range(3):
                dispatch(which, c, k).wait_send()
            for which in range(2):
                give_back(which, c, k).wait_send()


def local(
    act_prev,
    fwd_routes,
    fwd_gates,
    saved_input,
    grad_prev,
    bwd_routes,
    bwd_gates,
    norm_gain,
    w_up,
    w_down,
):
    n_pipe = lax.axis_size("pipe")
    n_x = 4
    n_experts = lax.axis_size("expert") // (2 * n_x)
    tokens, dim = act_prev.shape[1], act_prev.shape[2]
    hidden, width = w_up.shape[2], w_up.shape[3]
    cap = 3 * tokens // (2 * n_experts)
    blocks = dim // width
    chunks = blocks // 2
    slots = n_experts * cap
    bf16, f32 = jnp.bfloat16, jnp.float32
    dma = pltpu.SemaphoreType.DMA
    vmem, anywhere = pl.BlockSpec(memory_space=pltpu.VMEM), pl.BlockSpec(memory_space=pl.ANY)
    return pl.pallas_call(
        functools.partial(kernel, (n_pipe, n_experts, n_x, cap, chunks, width)),
        out_shape=[jax.ShapeDtypeStruct(act_prev.shape, bf16)] * 2,
        in_specs=[anywhere, vmem, vmem, vmem, anywhere, vmem, vmem, vmem, anywhere, anywhere],
        out_specs=[vmem, vmem],
        scratch_shapes=[
            pltpu.VMEM((tokens, dim), bf16),
            pltpu.VMEM((tokens, dim), bf16),
            pltpu.VMEM((blocks, hidden, width), bf16),
            pltpu.VMEM((blocks, hidden, width), bf16),
            pltpu.VMEM((tokens, dim), bf16),
            pltpu.VMEM((3, chunks, n_experts - 1, 2 * cap, width), bf16),
            pltpu.VMEM((3, chunks, n_experts, 2 * cap, width), bf16),
            pltpu.VMEM((2, chunks, n_experts - 1, 2 * cap, width), bf16),
            pltpu.VMEM((2, chunks, n_experts, 2 * cap, width), bf16),
            pltpu.VMEM((slots, hidden), f32),
            pltpu.VMEM((slots, hidden), f32),
            pltpu.VMEM((slots, hidden), bf16),
            pltpu.VMEM((tokens, dim), f32),
            dma((2,)),
            dma((2,)),
            dma((2, 13)),
            dma((2, 13)),
            dma((2,)),
            dma((3, chunks, n_experts - 1)),
            dma((3, chunks, n_experts - 1)),
            dma((2, chunks, n_experts - 1)),
            dma((2, chunks, n_experts - 1)),
        ],
        compiler_params=pltpu.CompilerParams(
            collective_id=0, has_side_effects=True, vmem_limit_bytes=48 * 2**20
        ),
        cost_estimate=pl.CostEstimate(
            flops=10 * slots * hidden * dim, bytes_accessed=24 * 2**20, transcendentals=0
        ),
    )(
        act_prev,
        fwd_routes,
        fwd_gates,
        saved_input,
        grad_prev,
        bwd_routes,
        bwd_gates,
        norm_gain,
        w_up,
        w_down,
    )


def solution(mesh):
    rows = P("pipe", "expert", None)
    blocks = P("pipe", "expert", None, None)
    return jax.shard_map(
        local,
        mesh=mesh,
        in_specs=(rows,) * 7 + (P("pipe", None), blocks, blocks),
        out_specs=(rows, rows),
        check_vma=False,
    )
```

time: 484 us -> 221 us (0.46)
  the two profiles are of different devices: /device:TPU:57 before, /device:TPU:1 now
where the time goes in v1:
time: 221 us
  Pallas kernels  210 us (95%)
  local copies, waits for them, and re-layouts  9.93 us (4%)
    pallas_call x1, Pallas kernels, local(): pl.pallas_call(functools.partial(kernel, (n_pipe, n_experts, n_x, cap, ch...  210 us
    unnamed x24, local copies, waits for them, and re-layouts  9.93 us

profile of v1, /device:TPU:1, one launch (start us, length us, event | category | flops | bytes accessed | tf_op | source)
XLA Modules:
  0.0 220.7 jit_solution(8534027435184976613)
XLA Ops:
  0.6 0.0 copy-start.6
  0.6 0.8 copy.12.fwd_routes_ref
  1.4 0.0 copy-done.6
  1.4 0.0 copy-start.7
  1.4 0.1 copy.13.fwd_gates_ref
  1.5 0.6 copy-done.7
  2.0 0.0 copy-start.8
  2.1 0.1 copy.14.bwd_routes_ref
  2.1 0.6 copy-done.8
  2.7 0.0 copy-start.5
  2.7 0.1 copy.15.bwd_gates_ref
  2.8 0.6 copy-done.5
  3.4 0.0 copy-start
  3.4 1.2 copy-done
  4.6 0.0 copy-start.1
  4.7 1.2 copy-done.1
  5.9 0.0 copy-start.2
  5.9 1.0 copy-done.2
  6.9 0.0 copy-start.3
  6.9 1.0 copy-done.3
  8.0 0.0 copy-start.4
  8.0 1.0 copy-done.4
  9.0 210.2 %shard_map.113 = (bf16[1,64,4096]{2,1,0:T(8,128)(2,1)S(1)}, bf16[1,64,4096]{2,1,0:T(8,128)(2,1)S(1)}) custom-call(bf16[1,64,4096]{2,1,0:T(8,128)(2,1)S(1)} %copy-done.2, s32[1,64,1]{2,1,0:T(8,128)S(1)} %copy.12.fwd_routes_ref, f32[1,64,1]{2,1,0:T(8,128)S(1)} %copy.13.fwd_gates_ref, bf16[1,64,4096]{2,1,0:T(8,128)(2,1)S(1)} %copy-done.3, ...), custom_call_target="tpu_custom_call" | custom-call | flops 4026531840 | bytes 25165824 | tf_op jit(solution)/shard_map/pallas_call | solution.py:378
  219.2 0.8 copy.18
  220.0 0.8 copy.19
Async XLA Ops:
  0.6 0.8 copy-start.6
  1.4 0.7 copy-start.7
  2.0 0.7 copy-start.8
  2.7 0.7 copy-start.5
  3.4 1.2 copy-start
  4.6 1.2 copy-start.1
  5.9 1.0 copy-start.2
  6.9 1.0 copy-start.3
  8.0 1.0 copy-start.4

commit v2 on v1

--- a/solution.py
+++ b/solution.py
@@ -14,12 +14,19 @@
 TRANS_RHS = (((1,), (1,)), ((), ()))
 
 
+def as_column(row):
+    n = row.shape[1]
+    down = lax.broadcasted_iota(jnp.int32, (n, n), 0)
+    across = lax.broadcasted_iota(jnp.int32, (n, n), 1)
+    return jnp.sum(jnp.where(down == across, row, 0.0), axis=1, keepdims=True)
+
+
 def slot_masks(routes, here, n_experts, capacity):
-    tokens = routes.shape[0]
-    relative = lax.rem(routes - here + n_experts, n_experts).astype(jnp.float32)
+    tokens = routes.shape[1]
+    as_row = lax.rem(routes - here + n_experts, n_experts).astype(jnp.float32)
+    relative = as_column(as_row)
     down = lax.broadcasted_iota(jnp.int32, (tokens, tokens), 0)
     across = lax.broadcasted_iota(jnp.int32, (tokens, tokens), 1)
-    as_row = jnp.sum(jnp.where(down == across, relative, 0.0), axis=0, keepdims=True)
     same = jnp.where(relative == as_row, 1.0, 0.0)
     rank_col = jnp.sum(jnp.where(across < down, same, 0.0), axis=1, keepdims=True)
     rank_row = jnp.sum(jnp.where(down < across, same, 0.0), axis=0, keepdims=True)
@@ -36,19 +43,26 @@
 def kernel(
     sizes,
     act_ref,
-    fwd_routes_ref,
-    fwd_gates_ref,
-    saved_ref,
+    fwd_routes_hbm,
+    fwd_gates_hbm,
+    saved_hbm,
     grad_ref,
-    bwd_routes_ref,
-    bwd_gates_ref,
-    gain_ref,
+    bwd_routes_hbm,
+    bwd_gates_hbm,
+    gain_hbm,
     up_ref,
     down_ref,
     out_ref,
     dx_ref,
+    fwd_routes_ref,
+    fwd_gates_ref,
+    saved_ref,
+    bwd_routes_ref,
+    bwd_gates_ref,
+    gain_ref,
     x_buf,
     gy_buf,
+    passing,
     up_all,
     down_all,
     normed,
@@ -60,8 +74,11 @@
     dact,
     mid,
     dn,
+    load_sem,
     pipe_send,
     pipe_recv,
+    relay_send,
+    relay_recv,
     w_send,
     w_recv,
     w_own,
@@ -70,7 +87,7 @@
     ret_send,
     ret_recv,
 ):
-    n_pipe, n_experts, n_x, cap, chunks, width = sizes
+    n_pipe, n_y, n_experts, n_x, cap, chunks, width = sizes
     tokens = saved_ref.shape[1]
     dim = saved_ref.shape[2]
     per_group = 2 * n_x
@@ -91,22 +108,119 @@
     sibling = (pipe, here * per_group + spot_of(my_x, 1 - core))
     later = (lax.rem(pipe + 1, n_pipe), place)
     earlier = (lax.rem(pipe + n_pipe - 1, n_pipe), place)
+    my_y, my_z = lax.rem(pipe, n_y), pipe // n_y
+    n_z = n_pipe // n_y
+
+    def at_yz(y, z):
+        return (lax.rem(z + n_z, n_z) * n_y + y, place)
 
     barrier = pltpu.get_barrier_semaphore()
-    peers = [right, left, sibling, later, earlier] + [group_peer(k) for k in range(1, n_experts)]
-    for peer in peers:
+
+    def greet(peer):
         pl.semaphore_signal(barrier, inc=1, device_id=peer, device_id_type=MESH)
 
-    def pipe_copy(i):
-        src, dst, peer = ((act_ref.at[0], x_buf, later), (grad_ref.at[0], gy_buf, earlier))[i]
+    for k in range(1, n_experts):
+        greet(group_peer(k))
+    for peer in (right, left, sibling):
+        greet(peer)
+    for k in range(1, n_y):
+        greet(at_yz(lax.rem(my_y + k, n_y), my_z))
+
+    @pl.when(my_y == 0)
+    def _():
+        for y in range(n_y):
+            greet(at_yz(y, my_z - 1))
+
+    @pl.when(my_y == n_y - 1)
+    def _():
+        for y in range(n_y):
+            greet(at_yz(y, my_z + 1))
+
+    greetings = (n_experts - 1) + 3 + (n_y - 1) + 2
+
+    loads = [
+        pltpu.make_async_copy(src, dst, load_sem.at[i])
+        for i, (src, dst) in enumerate(
+            (
+                (saved_hbm, saved_ref),
+                (gain_hbm, gain_ref),
+                (bwd_routes_hbm, bwd_routes_ref),
+                (bwd_gates_hbm, bwd_gates_ref),
+                (fwd_routes_hbm, fwd_routes_ref),
+                (fwd_gates_hbm, fwd_gates_ref),
+            )
+        )
+    ]
+    for load in loads:
+        load.start()
+
+    part = tokens // n_y
+    last_y = n_y - 1
+    crossing = (my_y == last_y, my_y == 0)
+    straight = (last_y, 0)
+    relays = (range(0, last_y), range(1, n_y))
+
+    def part_rows(y):
+        return pl.ds(y * part, part)
+
+    def remote(src, dst, send_sem, recv_sem, peer):
         return pltpu.make_async_remote_copy(
             src_ref=src,
             dst_ref=dst,
-            send_sem=pipe_send.at[i],
-            recv_sem=pipe_recv.at[i],
+            send_sem=send_sem,
+            recv_sem=recv_sem,
             device_id=peer,
             device_id_type=MESH,
         )
+
+    pipe_ends = ((act_ref, x_buf, later), (grad_ref, gy_buf, earlier))
+
+    def pipe_part(w, y):
+        src, dst, peer = pipe_ends[w]
+        rows = part_rows(y)
+        return remote(src.at[0, rows], dst.at[rows], pipe_send.at[w, y], pipe_recv.at[w, y], peer)
+
+    def pipe_to_relay(w, y):
+        src = pipe_ends[w][0].at[0, part_rows(y)]
+        return remote(src, passing.at[w], pipe_send.at[w, y], relay_recv.at[w], at_yz(y, my_z))
+
+    def pipe_from_relay(w, y):
+        peer = (at_yz(0, my_z + 1), at_yz(last_y, my_z - 1))[w]
+        dst = pipe_ends[w][1].at[part_rows(y)]
+        return remote(passing.at[w], dst, relay_send.at[w], pipe_recv.at[w, y], peer)
+
+    def pipe_start(w):
+        @pl.when(crossing[w])
+        def _():
+            for y in relays[w]:
+                pipe_to_relay(w, y).start()
+            pipe_part(w, straight[w]).start()
+
+        @pl.when(jnp.logical_not(crossing[w]))
+        def _():
+            for y in range(n_y):
+                pipe_part(w, y).start()
+
+    def pipe_pass_on(w):
+        for y in relays[w]:
+
+            @pl.when(my_y == y)
+            def _():
+                pipe_to_relay(w, y).wait_recv()
+                pipe_from_relay(w, y).start()
+
+    def pipe_arrived(w):
+        for y in range(n_y):
+            pipe_part(w, y).wait_recv()
+
+    def pipe_sent(w):
+        for y in range(n_y):
+            pipe_part(w, y).wait_send()
+        for y in relays[w]:
+
+            @pl.when(my_y == y)
+            def _():
+                pipe_from_relay(w, y).wait_send()
 
     def dispatch(which, c, k):
         return pltpu.make_async_remote_copy(
@@ -205,48 +319,55 @@
         for k in range(1, n_experts):
             dispatch(which, c, k).start()
 
-    def pack_and_send(which, pack):
-        @pl.loop(0, chunks)
-        def _(c):
-            pack_piece(which, c, pack)
-            send_piece(which, c)
-
     def scale_of(values):
         return lax.rsqrt(jnp.sum(values * values, axis=-1, keepdims=True) * (1.0 / dim) + EPS)
 
+    for load in loads:
+        load.wait()
     gain = gain_ref[...]
-
     saved = saved_ref[0].astype(jnp.float32)
     scale_b = scale_of(saved)
     normed[...] = (saved * scale_b * gain).astype(jnp.bfloat16)
-    gather_b, pack_b = slot_masks(bwd_routes_ref[0], here, n_experts, cap)
+    gather_b, pack_b = slot_masks(bwd_routes_ref[...], here, n_experts, cap)
 
     @pl.loop(0, chunks)
     def _(c):
         pack_piece(ROWS, c, pack_b)
 
-    pl.semaphore_wait(barrier, len(peers))
-
-    pipe_copy(1).start()
-    pipe_copy(0).start()
+    pl.semaphore_wait(barrier, greetings)
+
+    pipe_start(1)
+    pipe_start(0)
 
     @pl.loop(0, chunks)
     def _(c):
         send_piece(ROWS, c)
 
+    pipe_pass_on(1)
+    pipe_pass_on(0)
+
     for m in range(2):
         for i in (0, 3, 1, 2, 6):
             weight_copy(m, i).start()
 
-    pipe_copy(1).wait_recv()
-    normed[...] = (gy_buf[...].astype(jnp.float32) * bwd_gates_ref[0]).astype(jnp.bfloat16)
-    pack_and_send(COT, pack_b)
-
-    gather_f, pack_f = slot_masks(fwd_routes_ref[0], here, n_experts, cap)
-    pipe_copy(0).wait_recv()
+    gates_b = as_column(bwd_gates_ref[...])
+    pipe_arrived(1)
+    normed[...] = (gy_buf[...].astype(jnp.float32) * gates_b).astype(jnp.bfloat16)
+
+    @pl.loop(0, chunks)
+    def _(c):
+        pack_piece(COT, c, pack_b)
+        send_piece(COT, c)
+
+    gather_f, pack_f = slot_masks(fwd_routes_ref[...], here, n_experts, cap)
+    pipe_arrived(0)
     x = x_buf[...].astype(jnp.float32)
     normed[...] = (x * scale_of(x) * gain).astype(jnp.bfloat16)
-    pack_and_send(FWD, pack_f)
+
+    @pl.loop(0, chunks)
+    def _(c):
+        pack_piece(FWD, c, pack_f)
+        send_piece(FWD, c)
 
     def pass_on(m):
         weight_copy(m, 0).wait_recv()
@@ -328,7 +449,7 @@
         + (dn[...] * scale_b - saved_ref[0].astype(jnp.float32) * pull)
     ).astype(jnp.bfloat16)
 
-    gates = fwd_gates_ref[0]
+    gates = as_column(fwd_gates_ref[...])
 
     @pl.loop(0, chunks)
     def _(c):
@@ -336,8 +457,8 @@
             at = cols(2 * c + j)
             out_ref[0, :, at] = (x_buf[:, at].astype(jnp.float32) + e * gates).astype(jnp.bfloat16)
 
-    for i in range(2):
-        pipe_copy(i).wait_send()
+    for w in range(2):
+        pipe_sent(w)
     for m in range(2):
         for i in range(13):
             weight_copy(m, i).wait_send()
@@ -364,7 +485,7 @@
     w_down,
 ):
     n_pipe = lax.axis_size("pipe")
-    n_x = 4
+    n_x, n_y = 4, 4
     n_experts = lax.axis_size("expert") // (2 * n_x)
     tokens, dim = act_prev.shape[1], act_prev.shape[2]
     hidden, width = w_up.shape[2], w_up.shape[3]
@@ -374,15 +495,22 @@
     slots = n_experts * cap
     bf16, f32 = jnp.bfloat16, jnp.float32
     dma = pltpu.SemaphoreType.DMA
-    vmem, anywhere = pl.BlockSpec(memory_space=pltpu.VMEM), pl.BlockSpec(memory_space=pl.ANY)
+    vmem, hbm = pl.BlockSpec(memory_space=pltpu.VMEM), pl.BlockSpec(memory_space=pltpu.HBM)
     return pl.pallas_call(
-        functools.partial(kernel, (n_pipe, n_experts, n_x, cap, chunks, width)),
+        functools.partial(kernel, (n_pipe, n_y, n_experts, n_x, cap, chunks, width)),
         out_shape=[jax.ShapeDtypeStruct(act_prev.shape, bf16)] * 2,
-        in_specs=[anywhere, vmem, vmem, vmem, anywhere, vmem, vmem, vmem, anywhere, anywhere],
+        in_specs=[hbm] * 10,
         out_specs=[vmem, vmem],
         scratch_shapes=[
+            pltpu.VMEM((1, tokens), jnp.int32),
+            pltpu.VMEM((1, tokens), f32),
+            pltpu.VMEM((1, tokens, dim), bf16),
+            pltpu.VMEM((1, tokens), jnp.int32),
+            pltpu.VMEM((1, tokens), f32),
+            pltpu.VMEM((1, dim), f32),
             pltpu.VMEM((tokens, dim), bf16),
             pltpu.VMEM((tokens, dim), bf16),
+            pltpu.VMEM((2, tokens // n_y, dim), bf16),
             pltpu.VMEM((blocks, hidden, width), bf16),
             pltpu.VMEM((blocks, hidden, width), bf16),
             pltpu.VMEM((tokens, dim), bf16),
@@ -394,6 +522,9 @@
             pltpu.VMEM((slots, hidden), f32),
             pltpu.VMEM((slots, hidden), bf16),
             pltpu.VMEM((tokens, dim), f32),
+            dma((6,)),
+            dma((2, n_y)),
+            dma((2, n_y)),
             dma((2,)),
             dma((2,)),
             dma((2, 13)),
@@ -405,19 +536,19 @@
             dma((2, chunks, n_experts - 1)),
         ],
         compiler_params=pltpu.CompilerParams(
-            collective_id=0, has_side_effects=True, vmem_limit_bytes=48 * 2**20
+            collective_id=0, has_side_effects=True, vmem_limit_bytes=60 * 2**20
         ),
         cost_estimate=pl.CostEstimate(
             flops=10 * slots * hidden * dim, bytes_accessed=24 * 2**20, transcendentals=0
         ),
     )(
         act_prev,
-        fwd_routes,
-        fwd_gates,
+        fwd_routes.reshape(1, tokens),
+        fwd_gates.reshape(1, tokens),
         saved_input,
         grad_prev,
-        bwd_routes,
-        bwd_gates,
+        bwd_routes.reshape(1, tokens),
+        bwd_gates.reshape(1, tokens),
         norm_gain,
         w_up,
         w_down,

time: 221 us -> 205 us (0.928); the launches traced: 221 us -> 201 us
  Pallas kernels: 210 us -> 198 us
  local copies, waits for them, and re-layouts: 9.93 us -> 2.72 us
    pallas_call x1, Pallas kernels: 210 us -> 198 us  [local(): pl.pallas_call(functools.partial(kernel, (n_pipe, n_y, n_experts, n_x, ca...]
    unnamed x24 -> x4, local copies, waits for them, and re-layouts: 9.93 us -> 2.72 us
where the time goes in v2:
time: 205 us; the launch traced here: 201 us
  Pallas kernels  198 us (97%)
  local copies, waits for them, and re-layouts  2.72 us (1%)
    pallas_call x1, Pallas kernels, local(): pl.pallas_call(functools.partial(kernel, (n_pipe, n_y, n_experts, n_x, ca...  198 us

profile of v2, /device:TPU:1, one launch (start us, length us, event | category | flops | bytes accessed | tf_op | source)
XLA Modules:
  0.0 201.0 jit_solution(8858164852883242558)
XLA Ops:
  0.6 197.6 %shard_map.113 = (bf16[1,64,4096]{2,1,0:T(8,128)(2,1)}, bf16[1,64,4096]{2,1,0:T(8,128)(2,1)}) custom-call(bf16[1,64,4096]{2,1,0:T(8,128)(2,1)} %act_ref.1, s32[1,64]{1,0:T(1,128)} %bitcast.4, f32[1,64]{1,0:T(1,128)} %bitcast.5, bf16[1,64,4096]{2,1,0:T(8,128)(2,1)} %saved_hbm.1, bf16[1,64,4096]{2,1,0:T(8,128)(2,1)} %grad_ref.1, s32[1,64]{1,0:T(1,128)} %bitcast.6, ...), custom_call_target="tpu_custom_call" | custom-call | flops 4026531840 | bytes 25165824 | tf_op jit(solution)/shard_map/pallas_call | solution.py:499
  198.2 0.0 copy-start
  198.2 1.9 copy.14
  200.2 0.0 copy-done
  200.2 0.8 copy.15
Async XLA Ops:
  198.2 1.9 copy-start

commit v3 on v2

--- a/solution.py
+++ b/solution.py
@@ -330,25 +330,24 @@
     normed[...] = (saved * scale_b * gain).astype(jnp.bfloat16)
     gather_b, pack_b = slot_masks(bwd_routes_ref[...], here, n_experts, cap)
 
-    @pl.loop(0, chunks)
-    def _(c):
-        pack_piece(ROWS, c, pack_b)
-
+    pack_piece(ROWS, 0, pack_b)
     pl.semaphore_wait(barrier, greetings)
 
     pipe_start(1)
     pipe_start(0)
-
-    @pl.loop(0, chunks)
-    def _(c):
-        send_piece(ROWS, c)
-
-    pipe_pass_on(1)
-    pipe_pass_on(0)
-
+    send_piece(ROWS, 0)
     for m in range(2):
         for i in (0, 3, 1, 2, 6):
             weight_copy(m, i).start()
+    pipe_pass_on(1)
+
+    @pl.loop(1, chunks)
+    def _(c):
+        pack_piece(ROWS, c, pack_b)
+        send_piece(ROWS, c)
+
+    pipe_pass_on(0)
+
 
     gates_b = as_column(bwd_gates_ref[...])
     pipe_arrived(1)
@@ -536,7 +535,7 @@
             dma((2, chunks, n_experts - 1)),
         ],
         compiler_params=pltpu.CompilerParams(
-            collective_id=0, has_side_effects=True, vmem_limit_bytes=60 * 2**20
+            collective_id=0, has_side_effects=True, vmem_limit_bytes=105 * 2**19
         ),
         cost_estimate=pl.CostEstimate(
             flops=10 * slots * hidden * dim, bytes_accessed=24 * 2**20, transcendentals=0

time: 205 us -> 200 us (0.976); the launches traced: 201 us -> 199 us
  no operation moved by 1% of the time
where the time goes in v3:
time: 200 us; the launch traced here: 199 us
  Pallas kernels  196 us (98%)
  local copies, waits for them, and re-layouts  2.98 us (1%)
    pallas_call x1, Pallas kernels, local(): pl.pallas_call(functools.partial(kernel, (n_pipe, n_y, n_experts, n_x, ca...  196 us

profile of v3, /device:TPU:1, one launch (start us, length us, event | category | flops | bytes accessed | tf_op | source)
XLA Modules:
  0.0 199.5 jit_solution(4763365297272394896)
XLA Ops:
  0.6 0.0 copy-start.4
  0.6 0.0 copy-start.1
  0.7 0.0 copy-start.2
  0.7 0.0 copy-start.3
  0.7 0.6 copy-done.4
  1.3 0.0 copy-done.1
  1.3 0.0 copy-done.2
  1.3 0.0 copy-done.3
  1.3 0.0 copy-start
  1.3 0.7 copy-done
  2.1 195.8 %shard_map.113 = (bf16[1,64,4096]{2,1,0:T(8,128)(2,1)S(1)}, bf16[1,64,4096]{2,1,0:T(8,128)(2,1)S(1)}) custom-call(bf16[1,64,4096]{2,1,0:T(8,128)(2,1)} %act_ref.1, s32[1,64]{1,0:T(1,128)S(1)} %bitcast.4, f32[1,64]{1,0:T(1,128)S(1)} %bitcast.5, bf16[1,64,4096]{2,1,0:T(8,128)(2,1)} %saved_hbm.1, bf16[1,64,4096]{2,1,0:T(8,128)(2,1)} %grad_ref.1, ...), custom_call_target="tpu_custom_call" | custom-call | flops 4026531840 | bytes 25165824 | tf_op jit(solution)/shard_map/pallas_call | solution.py:498
  197.9 0.8 copy.14
  198.7 0.8 copy.15
Async XLA Ops:
  0.6 0.7 copy-start.4
  0.6 0.7 copy-start.1
  0.7 0.7 copy-start.2
  0.7 0.7 copy-start.3
  1.3 0.7 copy-start

commit v4 on v3

--- a/solution.py
+++ b/solution.py
@@ -535,22 +535,27 @@
             dma((2, chunks, n_experts - 1)),
         ],
         compiler_params=pltpu.CompilerParams(
-            collective_id=0, has_side_effects=True, vmem_limit_bytes=105 * 2**19
+            collective_id=0, has_side_effects=True, vmem_limit_bytes=48 * 2**20
         ),
         cost_estimate=pl.CostEstimate(
             flops=10 * slots * hidden * dim, bytes_accessed=24 * 2**20, transcendentals=0
         ),
     )(
-        act_prev,
-        fwd_routes.reshape(1, tokens),
-        fwd_gates.reshape(1, tokens),
-        saved_input,
-        grad_prev,
-        bwd_routes.reshape(1, tokens),
-        bwd_gates.reshape(1, tokens),
-        norm_gain,
-        w_up,
-        w_down,
+        *(
+            pltpu.with_memory_space_constraint(operand, pltpu.HBM)
+            for operand in (
+                act_prev,
+                fwd_routes.reshape(1, tokens),
+                fwd_gates.reshape(1, tokens),
+                saved_input,
+                grad_prev,
+                bwd_routes.reshape(1, tokens),
+                bwd_gates.reshape(1, tokens),
+                norm_gain,
+                w_up,
+                w_down,
+            )
+        )
     )
 
 

time: 200 us -> 198 us (0.990)
  no operation moved by 1% of the time
where the time goes in v4:
time: 198 us
  Pallas kernels  196 us (99%)
    pallas_call x1, Pallas kernels, local(): pl.pallas_call(functools.partial(kernel, (n_pipe, n_y, n_experts, n_x, ca...  196 us

profile of v4, /device:TPU:1, one launch (start us, length us, event | category | flops | bytes accessed | tf_op | source)
XLA Modules:
  0.0 198.1 jit_solution(9835022205513578650)
XLA Ops:
  0.6 195.8 %shard_map.113 = (bf16[1,64,4096]{2,1,0:T(8,128)(2,1)S(1)}, bf16[1,64,4096]{2,1,0:T(8,128)(2,1)S(1)}) custom-call(bf16[1,64,4096]{2,1,0:T(8,128)(2,1)} %act_ref.1, s32[1,64]{1,0:T(1,128)} %bitcast.4, f32[1,64]{1,0:T(1,128)} %bitcast.5, bf16[1,64,4096]{2,1,0:T(8,128)(2,1)} %saved_hbm.1, bf16[1,64,4096]{2,1,0:T(8,128)(2,1)} %grad_ref.1, s32[1,64]{1,0:T(1,128)} %bitcast.6, ...), custom_call_target="tpu_custom_call" | custom-call | flops 4026531840 | bytes 25165824 | tf_op jit(solution)/shard_map/pallas_call | solution.py:498
  196.5 0.8 copy.14
  197.3 0.8 copy.15

commit v5 on v4

--- a/solution.py
+++ b/solution.py
@@ -448,6 +448,19 @@
         + (dn[...] * scale_b - saved_ref[0].astype(jnp.float32) * pull)
     ).astype(jnp.bfloat16)
 
+    for w in range(2):
+        pipe_sent(w)
+    for m in range(2):
+        for i in range(13):
+            weight_copy(m, i).wait_send()
+
+    @pl.loop(0, chunks)
+    def _(c):
+        for k in range(1, n_experts):
+            for which in range(3):
+                dispatch(which, c, k).wait_send()
+            give_back(DROW, c, k).wait_send()
+
     gates = as_column(fwd_gates_ref[...])
 
     @pl.loop(0, chunks)
@@ -456,19 +469,10 @@
             at = cols(2 * c + j)
             out_ref[0, :, at] = (x_buf[:, at].astype(jnp.float32) + e * gates).astype(jnp.bfloat16)
 
-    for w in range(2):
-        pipe_sent(w)
-    for m in range(2):
-        for i in range(13):
-            weight_copy(m, i).wait_send()
-
     @pl.loop(0, chunks)
     def _(c):
         for k in range(1, n_experts):
-            for which in range(3):
-                dispatch(which, c, k).wait_send()
-            for which in range(2):
-                give_back(which, c, k).wait_send()
+            give_back(EOUT, c, k).wait_send()
 
 
 def local(

time: 198 us -> 198 us (level)
  no operation moved by 1% of the time
where the time goes in v5:
time: 198 us
  Pallas kernels  196 us (99%)
    pallas_call x1, Pallas kernels, local(): pl.pallas_call(functools.partial(kernel, (n_pipe, n_y, n_experts, n_x, ca...  196 us

profile of v5, /device:TPU:1, one launch (start us, length us, event | category | flops | bytes accessed | tf_op | source)
XLA Modules:
  0.0 197.9 jit_solution(16846975364409384784)
XLA Ops:
  0.6 195.7 %shard_map.113 = (bf16[1,64,4096]{2,1,0:T(8,128)(2,1)S(1)}, bf16[1,64,4096]{2,1,0:T(8,128)(2,1)S(1)}) custom-call(bf16[1,64,4096]{2,1,0:T(8,128)(2,1)} %act_ref.1, s32[1,64]{1,0:T(1,128)} %bitcast.4, f32[1,64]{1,0:T(1,128)} %bitcast.5, bf16[1,64,4096]{2,1,0:T(8,128)(2,1)} %saved_hbm.1, bf16[1,64,4096]{2,1,0:T(8,128)(2,1)} %grad_ref.1, s32[1,64]{1,0:T(1,128)} %bitcast.6, ...), custom_call_target="tpu_custom_call" | custom-call | flops 4026531840 | bytes 25165824 | tf_op jit(solution)/shard_map/pallas_call | solution.py:502
  196.4 0.8 copy.14
  197.2 0.8 copy.15
